TPU v7x, 32 devices: a whole 2x2x4 slice. The times are simulated.
32 devices in a mesh: cfg: 1, node: 32 (over z, y, x, core), pair: 1.
Axes of the slice: x: 2, y: 2, z: 4, core: 2. Of those that a mesh axis runs over, the one named last changes fastest.
Arguments:
- node_blocks: float32 [256, 2, 256, 256], P(('cfg', 'node'), None, None, 'pair'), may hold values from -1.5 to 1.5
- node_slot: int32 [256], replicated, may hold values from 0 to 255, as said below
- pair_list: int32 [128, 2], replicated, may hold values from 0 to 255, as said below
- second_list: int32 [128, 2], replicated, may hold values from 0 to 127, as said below
- targets: int32 [128], replicated, may hold values from 0 to 63, as said below
- spin_signs: int32 [128], replicated, may hold values from -1 to 1, as said below
Outputs:
- results: float32 [64, 2, 256, 256], P(('cfg', 'node'), None, None, 'pair')
Inputs may be any that keep to these rules, and one draw needn't show every extreme that they name: `node_slot`: A permutation of the slots. `pair_list`: rows b * 4 to (b + 1) * 4 - 1 form block b. The first node of a pair in block b sits at a slot of b * 8 to (b + 1) * 8 - 1. For every block b and every owner o, at most 1 pair of block b has its second node at slots o * 8 to (o + 1) * 8 - 1; one owner supplies exactly 1 such node to every block. `second_list`: rows b * 4 to (b + 1) * 4 - 1 form block b. The first pair of a product in block b lies in block b of the pairs. For every block b and owner o, at most 1 product of block b has its second pair in block o of the pairs; one owner supplies exactly 1 such pair product to every block. `targets`: products of block b target results b * 2 to (b + 1) * 2 - 1. `spin_signs`: each entry is -1 or 1.
All inputs are finite; a program needn't handle non-finite values.
Results may differ from a plain program's by a relative error of at most 0.000098.
Values sent between devices are 32-bit elements; how exact they have to be, the bound alone decides.
A program may use at most 128 MiB of HBM per device.

v0:
```python
import jax
import jax.numpy as jnp
from jax import lax
from jax.sharding import PartitionSpec as P

NODE_COL = 8
PAIR_COL = 4
RES_COL = 2


def complex_product(left_side, right_side):
    half_width = right_side.shape[3]
    stacked_left = jnp.concatenate([left_side[:, 0], left_side[:, 1]], axis=2)
    real_right = jnp.concatenate([right_side[:, 0], -right_side[:, 1]], axis=1)
    imag_right = jnp.concatenate([right_side[:, 1], right_side[:, 0]], axis=1)
    stacked_right = jnp.concatenate([real_right, imag_right], axis=2)
    joined = jnp.einsum(
        "jmk,jkn->jmn",
        stacked_left,
        stacked_right,
        precision=lax.Precision.HIGHEST,
        preferred_element_type=jnp.float32,
    )
    return jnp.stack([joined[:, :, :half_width], joined[:, :, half_width:]], axis=1)


def send_table(owner_of, local_of, owner_now, capacity):
    matches = (owner_of == owner_now).astype(jnp.int32)
    ranking = jnp.cumsum(matches, axis=1) - 1
    levels = jnp.arange(capacity, dtype=jnp.int32)
    chosen = matches[:, None, :] * (ranking[:, None, :] == levels[None, :, None]).astype(jnp.int32)
    slot_index = jnp.sum(chosen * local_of[:, None, :], axis=2)
    present = jnp.sum(chosen, axis=2)
    return (slot_index.reshape(-1), present.reshape(-1))


def pack_items(local_items, owner_of, local_of, owner_now, capacity):
    slot_index, present = send_table(owner_of, local_of, owner_now, capacity)
    picked = jnp.take(local_items, slot_index, axis=0)
    return picked * present.astype(local_items.dtype)[:, None, None, None]


def receive_index(own_owner, capacity):
    item_count = own_owner.shape[0]
    earlier = jnp.arange(item_count)[:, None] > jnp.arange(item_count)[None, :]
    same_owner = own_owner[:, None] == own_owner[None, :]
    ranking = jnp.sum((earlier & same_owner).astype(jnp.int32), axis=1)
    return own_owner * capacity + ranking


def per_device(node_blocks, node_slot, pair_list, second_list, targets, spin_signs):
    columns = lax.axis_size("node")
    column = lax.axis_index("node")
    capacity = -(-PAIR_COL // columns)
    block_start = column * PAIR_COL
    own_pairs = lax.dynamic_slice_in_dim(pair_list, block_start, PAIR_COL, 0)
    first_slot = node_slot[own_pairs[:, 0]] - column * NODE_COL
    second_slot = node_slot[own_pairs[:, 1]]
    whole_nodes = lax.all_gather(node_blocks, "pair", axis=3, tiled=True)
    first_nodes = jnp.take(whole_nodes, first_slot, axis=0)
    every_slot = node_slot[pair_list[:, 1]].reshape(columns, PAIR_COL)
    outgoing = pack_items(
        node_blocks, every_slot // NODE_COL, every_slot % NODE_COL, column, capacity
    )
    incoming = lax.all_to_all(outgoing, "node", split_axis=0, concat_axis=0, tiled=True)
    second_nodes = jnp.take(incoming, receive_index(second_slot // NODE_COL, capacity), axis=0)
    products = complex_product(first_nodes, second_nodes)
    whole_products = lax.all_gather(products, "pair", axis=3, tiled=True)
    own_seconds = lax.dynamic_slice_in_dim(second_list, block_start, PAIR_COL, 0)
    left_side = jnp.take(whole_products, own_seconds[:, 0] - block_start, axis=0)
    every_right = second_list[:, 1].reshape(columns, PAIR_COL)
    outgoing_products = pack_items(
        products, every_right // PAIR_COL, every_right % PAIR_COL, column, capacity
    )
    incoming_products = lax.all_to_all(
        outgoing_products, "node", split_axis=0, concat_axis=0, tiled=True
    )
    right_side = jnp.take(
        incoming_products, receive_index(own_seconds[:, 1] // PAIR_COL, capacity), axis=0
    )
    own_signs = lax.dynamic_slice_in_dim(spin_signs, block_start, PAIR_COL, 0).astype(jnp.float32)
    seconds = complex_product(left_side, right_side) * own_signs[:, None, None, None]
    own_targets = lax.dynamic_slice_in_dim(targets, block_start, PAIR_COL, 0) - column * RES_COL
    selector = (own_targets[None, :] == jnp.arange(RES_COL)[:, None]).astype(jnp.float32)
    return jnp.einsum(
        "rj,jxmn->rxmn",
        selector,
        seconds,
        precision=lax.Precision.HIGHEST,
        preferred_element_type=jnp.float32,
    )


def solution(mesh):
    placed = (P(("cfg", "node"), None, None, "pair"), P(), P(), P(), P(), P())
    return jax.shard_map(
        per_device,
        mesh=mesh,
        in_specs=placed,
        out_specs=P(("cfg", "node"), None, None, "pair"),
        check_vma=False,
    )
```

profile of v0, /device:TPU:0, one launch (start us, length us, event | category | flops | bytes accessed | tf_op | source)
XLA Modules:
  0.0 830.8 jit_solution(6682804246031589908)
XLA Ops:
  0.0 0.7 slice_reduce_fusion
  0.7 0.1 reshape_squeeze.3
  0.8 0.2 reduce_window_sum.18
  1.0 0.1 fusion.38
  1.1 0.7 fusion.47
  1.8 1.3 gather_fusion.2
  3.1 0.1 reshape.175
  3.2 0.2 reduce_window_sum.17
  3.4 0.1 fusion.39
  3.6 10.0 %gather_fusion.3 = f32[32,2,256,256]{3,2,1,0:T(8,128)} fusion(f32[8,2,256,256]{3,2,1,0:T(8,128)} %param.8, s32[1024]{0:T(1024)S(1)} %pad_clamp_fusion.4), kind=kCustom, calls=%fused_computation.5 | custom fusion | bytes 33554560 | tf_op jit(solution)/shard_map/jit(_take)/gather | solution.py:39
  13.6 11.7 %select_multiply_fusion.1 = f32[32,2,256,256]{3,2,1,0:T(8,128)} fusion(f32[32,2,256,256]{3,2,1,0:T(8,128)} %gather_fusion.3, f32[32]{0:T(128)S(1)} %convert_element_type.47, pred[32]{0:T(512)(128)(4,1)S(1)} %get-tuple-element.33), kind=kLoop, calls=%fused_computation.10 | loop fusion | flops 8388608 | bytes 33554592 | tf_op jit(solution)/shard_map/mul | solution.py:40
  25.3 7.4 all-to-all-start
  32.8 0.1 constant_dynamic-slice_fusion
  32.9 0.6 gather_fusion.4
  33.5 0.6 gather_fusion
  34.3 2.9 gather_fusion.1
  37.2 0.2 convert_reduce_fusion.1
  37.4 0.2 copy_select_fusion.2
  37.7 1.1 slice_bitcast_fusion.11
  38.8 366.7 %all-to-all-done = f32[32,2,256,256]{3,2,1,0:T(8,128)} async-done(((f32[32,2,256,256]{3,2,1,0:T(8,128)}), f32[32,2,256,256]{3,2,1,0:T(8,128)}, u32[]{:S(2)}, u32[]{:S(2)}) %all-to-all-start) | async-done | bytes 16777248 | tf_op jit(solution)/shard_map/all_to_all | solution.py:65
  405.5 6.4 gather_fusion.7
  411.9 0.2 copy_select_fusion.1
  412.2 0.1 slice_bitcast_fusion.8
  412.3 0.1 fusion.55
  412.4 1.1 copy-done.2
  413.5 3.7 fusion
  417.3 0.2 slice_bitcast_fusion.7
  417.5 0.1 pad_maximum_fusion
  417.6 7.8 gather_fusion.6
  425.4 11.7 %select_multiply_fusion = f32[32,2,256,256]{3,2,1,0:T(8,128)} fusion(f32[32,2,256,256]{3,2,1,0:T(8,128)} %gather_fusion.6, f32[32]{0:T(128)S(1)} %convert_element_type.50, pred[32]{0:T(512)(128)(4,1)S(1)} %get-tuple-element.32), kind=kLoop, calls=%fused_computation.9 | loop fusion | flops 8388608 | bytes 33554592 | tf_op jit(solution)/shard_map/mul | solution.py:40
  437.1 4.2 all-to-all-start.1
  441.3 0.1 dynamic-slice_convert_fusion
  441.4 0.2 convert_reduce_fusion
  441.6 1.5 copy.19
  443.2 2.3 gather_fusion.5
  445.5 0.2 copy_select_fusion
  445.7 1.1 slice_bitcast_fusion.5
  446.8 367.4 %all-to-all-done.1 = f32[32,2,256,256]{3,2,1,0:T(8,128)} async-done(((f32[32,2,256,256]{3,2,1,0:T(8,128)}), f32[32,2,256,256]{3,2,1,0:T(8,128)}, u32[]{:S(2)}, u32[]{:S(2)}) %all-to-all-start.1) | async-done | bytes 16777248 | tf_op jit(solution)/shard_map/all_to_all | solution.py:75
  814.2 6.4 gather_fusion.8
  820.6 0.2 broadcast_select_fusion
  820.9 0.1 slice_bitcast_fusion.2
  821.0 0.1 fusion.56
  821.1 1.1 copy-done.3
  822.3 3.7 fusion.8
  826.0 0.2 slice_bitcast_fusion.1
  826.2 0.2 maximum_multiply_fusion
  826.5 3.2 fusion.22
  829.7 1.1 copy.23
  (37 shorter events, 0.3 us)
Async XLA Ops:
  0.0 1.8 copy-start
  25.3 7.4 copy-start.4
  25.3 8.8 %copy-start.5 = (s32[128,2]{0,1:T(2,128)S(1)}, s32[128,2]{0,1:T(2,128)}, u32[]{:S(2)}) copy-start(s32[128,2]{0,1:T(2,128)} %param.11) | copy-start | bytes 3076
  25.3 380.1 %all-to-all-start = ((f32[32,2,256,256]{3,2,1,0:T(8,128)}), f32[32,2,256,256]{3,2,1,0:T(8,128)}, u32[]{:S(2)}, u32[]{:S(2)}) async-start(f32[32,2,256,256]{3,2,1,0:T(8,128)} %select_multiply_fusion.1), calls=%async_computation | async-start | bytes 33554432 | tf_op jit(solution)/shard_map/all_to_all | solution.py:65
  412.3 1.2 copy-start.2
  437.1 4.2 copy-start.6
  437.1 4.2 copy-start.7
  437.1 377.1 %all-to-all-start.1 = ((f32[32,2,256,256]{3,2,1,0:T(8,128)}), f32[32,2,256,256]{3,2,1,0:T(8,128)}, u32[]{:S(2)}, u32[]{:S(2)}) async-start(f32[32,2,256,256]{3,2,1,0:T(8,128)} %select_multiply_fusion), calls=%async_computation.1 | async-start | bytes 33554432 | tf_op jit(solution)/shard_map/all_to_all | solution.py:75
  821.0 1.2 copy-start.3
  826.4 4.3 copy-start.1
where the time goes:
time: 831 us
  waiting for transfers between devices  734 us (88%)
  local copies, waits for them, and re-layouts  47.2 us (6%)
  other arithmetic  26.8 us (3%)
  starting transfers between devices  11.6 us (1%)
  matrix products  10.7 us (1%)
    all_to_all x1, waiting for transfers between devices, per_device(): lax.all_to_all(outgoing_products, 'node', split_axis=0, concat_axis=0, ti...  367 us
    all_to_all x1, waiting for transfers between devices, per_device(): lax.all_to_all(outgoing, 'node', split_axis=0, concat_axis=0, tiled=True)  367 us
    mul x2, other arithmetic, pack_items(): return picked * present.astype(local_items.dtype)[:, None, None, None]  23.4 us
    gather x2, local copies, waits for them, and re-layouts, pack_items(): picked = jnp.take(local_items, slot_index, axis=0)  17.8 us
  transfers between devices with their start and end apart: 2, of which 2 were waited for; matrix products, arithmetic and copies ran while one was open for 1% of the time, Pallas kernels for 0%

commit v1 on v0

v1 whole, which is shorter than its diff:
```python
import math

import jax
import jax.numpy as jnp
from jax import lax
from jax.sharding import PartitionSpec as P

GROUP = 8
STEPS = (8, 9, 10, 12)
RES_COL = 2


def complex_product(left_side, right_side):
    half_width = right_side.shape[3]
    stacked_left = jnp.concatenate([left_side[:, 0], left_side[:, 1]], axis=2)
    real_right = jnp.concatenate([right_side[:, 0], -right_side[:, 1]], axis=1)
    imag_right = jnp.concatenate([right_side[:, 1], right_side[:, 0]], axis=1)
    stacked_right = jnp.concatenate([real_right, imag_right], axis=2)
    joined = jnp.einsum(
        "jmk,jkn->jmn",
        stacked_left,
        stacked_right,
        precision=lax.Precision.HIGH,
        preferred_element_type=jnp.float32,
    )
    return jnp.stack([joined[:, :, :half_width], joined[:, :, half_width:]], axis=1)


def fetch(items, wanted, columns, column):
    count, _, rows, width = items.shape
    picks = wanted.shape[1]
    lanes = math.gcd(GROUP, columns)
    planes = columns // lanes
    plane, lane = column // lanes, column % lanes
    part = rows // lanes
    in_plane = [[p * lanes + q for q in range(lanes)] for p in range(planes)]
    in_line = [[p * lanes + q for p in range(planes)] for q in range(lanes)]
    held = lanes * count
    share = -(-count // planes)

    owners = wanted // count
    supplied = jnp.sum((owners.reshape(-1)[:, None] == jnp.arange(columns)[None, :]).astype(jnp.int32), axis=0)
    common = jnp.argmax(supplied).astype(jnp.int32)
    common_plane, common_lane = common // lanes, common % lanes
    is_common = owners == common

    flat = jnp.where(is_common, -1, wanted).reshape(planes, lanes * picks)
    need = jnp.any(flat[:, :, None] == jnp.arange(planes * held)[None, None, :], axis=1)
    need = need.reshape(planes, planes, held).transpose(1, 2, 0)
    foreign = jnp.arange(planes)[:, None] != jnp.arange(planes)[None, :]
    need = need & foreign[:, None, :]
    counted = need.astype(jnp.int32)
    lower = (jnp.arange(held)[:, None] > jnp.arange(held)[None, :]).astype(jnp.int32)
    rank = jnp.sum(lower[None, :, :, None] * counted[:, None, :, :], axis=2)
    most = jnp.max(jnp.sum(counted, axis=1))

    cut = items.reshape(count, 2, lanes, part, width).transpose(2, 0, 1, 3, 4)
    pieces = lax.all_to_all(cut, "node", 0, 0, axis_index_groups=in_plane, tiled=True)
    pieces = pieces.reshape(held, 2, part, width)

    mine = lax.dynamic_index_in_dim(counted, plane, 0, keepdims=False)
    my_rank = lax.dynamic_index_in_dim(rank, plane, 0, keepdims=False)
    to_me = lax.dynamic_index_in_dim(rank, plane, 2, keepdims=False)
    asked = lax.dynamic_slice_in_dim(wanted, plane * lanes, lanes, 0)
    asked_plane, asked_item = asked // held, asked % held
    asked_common = (asked // count) == common
    asked_rank = to_me[asked_plane, asked_item]
    shares = jnp.minimum(jnp.arange(planes * share), count - 1).reshape(planes, share)

    def across(capacity):
        def run(pieces):
            chosen = mine[:, :, None] * (my_rank[:, :, None] == jnp.arange(capacity)).astype(jnp.int32)
            listed = jnp.sum(chosen * jnp.arange(held)[:, None, None], axis=0)
            listed = jnp.concatenate([listed, common_lane * count + shares], axis=1)
            size = capacity + share
            packed = jnp.take(pieces, listed.reshape(-1), axis=0).reshape(planes, size, 2, part, width)
            came = lax.all_to_all(packed, "node", 0, 0, axis_index_groups=in_line, tiled=True)
            own_share = lax.dynamic_index_in_dim(came, common_plane, 0, keepdims=False)[capacity:]
            all_common = lax.all_gather(own_share, "node", axis=0, axis_index_groups=in_line, tiled=True)
            store = jnp.concatenate([pieces, came.reshape(planes * size, 2, part, width), all_common], axis=0)
            at = jnp.where(asked_plane == plane, asked_item, held + asked_plane * size + asked_rank)
            at = jnp.where(asked_common, held + planes * size + asked % count, at)
            return jnp.take(store, at.reshape(-1), axis=0)

        return run

    capacities = [c for c in STEPS if c < min(held, lanes * picks)] + [min(held, lanes * picks)]
    branch = jnp.sum((most > jnp.array(capacities[:-1], jnp.int32)).astype(jnp.int32))
    outgoing = lax.switch(branch, [across(c) for c in capacities], pieces)
    outgoing = outgoing.reshape(lanes, picks, 2, part, width)
    arrived = lax.all_to_all(outgoing, "node", 0, 0, axis_index_groups=in_plane, tiled=True)
    return arrived.transpose(1, 2, 0, 3, 4).reshape(picks, 2, rows, width)


def per_device(node_blocks, node_slot, pair_list, second_list, targets, spin_signs):
    columns = lax.axis_size("node")
    column = lax.axis_index("node")
    node_col = node_blocks.shape[0]
    pair_col = pair_list.shape[0] // columns
    block_start = column * pair_col
    own_pairs = lax.dynamic_slice_in_dim(pair_list, block_start, pair_col, 0)
    first_slot = node_slot[own_pairs[:, 0]] - column * node_col
    whole_nodes = lax.all_gather(node_blocks, "pair", axis=3, tiled=True)
    first_nodes = jnp.take(whole_nodes, first_slot, axis=0)
    wanted = node_slot[pair_list[:, 1]].reshape(columns, pair_col)
    second_nodes = fetch(node_blocks, wanted, columns, column)
    products = complex_product(first_nodes, second_nodes)
    whole_products = lax.all_gather(products, "pair", axis=3, tiled=True)
    own_seconds = lax.dynamic_slice_in_dim(second_list, block_start, pair_col, 0)
    left_side = jnp.take(whole_products, own_seconds[:, 0] - block_start, axis=0)
    right_side = fetch(products, second_list[:, 1].reshape(columns, pair_col), columns, column)
    own_signs = lax.dynamic_slice_in_dim(spin_signs, block_start, pair_col, 0).astype(jnp.float32)
    seconds = complex_product(left_side, right_side) * own_signs[:, None, None, None]
    return seconds, column


def solution(mesh):
    placed = (P(("cfg", "node"), None, None, "pair"), P(), P(), P(), P(), P())

    def run(node_blocks, node_slot, pair_list, second_list, targets, spin_signs):
        res_col = RES_COL

        def body(*args):
            seconds, column = per_device(*args)
            pair_col = seconds.shape[0]
            own = lax.dynamic_slice_in_dim(args[4], column * pair_col, pair_col, 0) - column * res_col
            return jnp.stack(
                [
                    jnp.sum(jnp.where((own == r)[:, None, None, None], seconds, 0.0), axis=0)
                    for r in range(res_col)
                ]
            )

        return jax.shard_map(
            body, mesh=mesh, in_specs=placed, out_specs=P(("cfg", "node"), None, None, "pair"), check_vma=False
        )(node_blocks, node_slot, pair_list, second_list, targets, spin_signs)

    return run
```

time: 831 us -> 367 us (0.44)
  waiting for transfers between devices: 734 us -> 211 us
  blocking collectives: 0 us -> 29.4 us
  starting transfers between devices: 11.6 us -> 30.9 us
  other arithmetic: 26.8 us -> 36.4 us
    all_to_all x2 -> x6, waiting for transfers between devices: 734 us -> 211 us  [the longest x2 118 us: run(): lax.all_to_all(packed, 'node', 0, 0, axis_index_groups=in_line, tiled=True)]
    all_gather x0 -> x2, blocking collectives: none -> 29.4 us  [run(): lax.all_gather(own_share, 'node', axis=0, axis_index_groups=in_line, tile...]
    mul x3 -> x0, other arithmetic: 23.6 us -> none  [the longest x2 23.4 us: pack_items(): return picked * present.astype(local_items.dtype)[:, None, None, None]]
    all_to_all x2 -> x6, starting transfers between devices: 11.6 us -> 30.9 us  [the longest x2 11.1 us: fetch(): lax.all_to_all(outgoing, 'node', 0, 0, axis_index_groups=in_plane, tiled=...]
    gather x7 -> x10, local copies, waits for them, and re-layouts: 33.3 us -> 15.7 us  [the longest x2 6.93 us: run(): return jnp.take(store, at.reshape(-1), axis=0)]
    reshape x1 -> x13, local copies, waits for them, and re-layouts: 0.09 us -> 11.9 us  [the longest x2 6.38 us: fetch(): outgoing = outgoing.reshape(lanes, picks, 2, part, width)]
    concatenate x0 -> x2, other arithmetic: none -> 10.1 us  [run(): jnp.concatenate([pieces, came.reshape(planes * size, 2, part, width), all...]
    select_n x6 -> x16, other arithmetic: 1.2 us -> 9.59 us  [the longest x4 5.33 us: run(): jnp.take(pieces, listed.reshape(-1), axis=0)]
  transfers between devices with their start and end apart: 2 -> 6, of which waited for: 2 -> 6; matrix products, arithmetic and copies ran while one was open for 1% -> 8% of each run, Pallas kernels for 0% -> 0%
where the time goes in v1:
time: 367 us; the launch traced here: 366 us
  waiting for transfers between devices  211 us (57%)
  local copies, waits for them, and re-layouts  46.5 us (13%)
  other arithmetic  36.4 us (10%)
  starting transfers between devices  30.9 us (8%)
  blocking collectives  29.4 us (8%)
  between operations  6.26 us (2%)
  matrix products  4.96 us (1%)
    all_to_all x2, waiting for transfers between devices, run(): lax.all_to_all(packed, 'node', 0, 0, axis_index_groups=in_line, tiled=True)  118 us
    all_to_all x2, waiting for transfers between devices, fetch(): lax.all_to_all(cut, 'node', 0, 0, axis_index_groups=in_plane, tiled=True)  57.3 us
    all_to_all x2, waiting for transfers between devices, fetch(): lax.all_to_all(outgoing, 'node', 0, 0, axis_index_groups=in_plane, tiled=...  35.6 us
    all_gather x2, blocking collectives, run(): lax.all_gather(own_share, 'node', axis=0, axis_index_groups=in_line, tile...  29.4 us
    all_to_all x2, starting transfers between devices, fetch(): lax.all_to_all(outgoing, 'node', 0, 0, axis_index_groups=in_plane, tiled=...  11.1 us
    all_to_all x2, starting transfers between devices, run(): lax.all_to_all(packed, 'node', 0, 0, axis_index_groups=in_line, tiled=True)  10.2 us
    concatenate x2, other arithmetic, run(): jnp.concatenate([pieces, came.reshape(planes * size, 2, part, width), all...  10.1 us
    all_to_all x2, starting transfers between devices, fetch(): lax.all_to_all(cut, 'node', 0, 0, axis_index_groups=in_plane, tiled=True)  9.64 us
  transfers between devices with their start and end apart: 6, of which 6 were waited for; matrix products, arithmetic and copies ran while one was open for 8% of the time, Pallas kernels for 0%

profile of v1, /device:TPU:0, one launch (start us, length us, event | category | flops | bytes accessed | tf_op | source)
XLA Modules:
  0.0 366.0 jit_solution(1427465301541051400)
XLA Ops:
  0.0 4.7 %copy.239 = f32[8,2,8,32,256]{4,3,1,0,2:T(8,128)} copy(f32[8,2,8,32,256]{4,3,2,1,0:T(8,128)} %bitcast.183) | data formatting | bytes 8388608 | tf_op jit(solution)/shard_map/reshape | solution.py:57
  4.7 5.3 %all-to-all-start.10 = ((f32[8,8,2,32,256]{4,3,2,1,0:T(8,128)}), f32[8,8,2,32,256]{4,3,2,1,0:T(8,128)}, u32[]{:S(2)}, u32[]{:S(2)}) async-start(f32[8,8,2,32,256]{4,3,2,1,0:T(8,128)} %bitcast.168), calls=%async_computation.10 | async-start | bytes 8388608 | tf_op jit(solution)/shard_map/all_to_all | solution.py:58
  10.1 1.3 gather_fusion.22
  15.7 1.2 fusion.101
  21.1 1.9 fusion.106
  23.7 35.6 %all-to-all-done.10 = f32[8,8,2,32,256]{4,3,2,1,0:T(8,128)} async-done(((f32[8,8,2,32,256]{4,3,2,1,0:T(8,128)}), f32[8,8,2,32,256]{4,3,2,1,0:T(8,128)}, u32[]{:S(2)}, u32[]{:S(2)}) %all-to-all-start.10) | async-done | bytes 4194336 | tf_op jit(solution)/shard_map/all_to_all | solution.py:58
  59.2 99.3 %conditional.2 = (f32[32,2,32,256]{3,2,1,0:T(8,128)}) conditional(s32[]{:T(128)} %clamp.6, (s32[8,4]{1,0:T(8,128)S(1)}, s32[]{:T(128)}, s32[8,4]{1,0:T(8,128)S(1)}, s32[8,4]{1,0:T(8,128)S(1)}, s32[8,4]{1,0:T(8,128)S(1)}, /*index=5*/pred[8,4]{1,0:T(8,128)(4,1)S(1)}, s32[64,4]{0,1:T(4,128)S(1)}, s32[64,4]{0,1:T(4,128)S(1)}, ...), branch_computations={%region_7.9_spmd, %region_9.11_spmd, %region_11.13_spmd, %region_1... | conditional | flops 9605181 | bytes 98976792 | solution.py:89
  59.8 2.9 gather_fusion.2
  62.7 1.8 broadcast_select_fusion.2
  64.5 5.6 %all-to-all-start.1 = ((f32[4,11,2,32,256]{4,3,2,1,0:T(8,128)}), f32[4,11,2,32,256]{4,3,2,1,0:T(8,128)S(1)}, u32[]{:S(2)}, u32[]{:S(2)}) async-start(f32[4,11,2,32,256]{4,3,2,1,0:T(8,128)} %broadcast_select_fusion.2), calls=%async_computation.1 | async-start | bytes 5767168 | tf_op jit(solution)/shard_map/cond/branch_1_fun/all_to_all | solution.py:77
  70.4 61.9 %all-to-all-done.1 = f32[4,11,2,32,256]{4,3,2,1,0:T(8,128)S(1)} async-done(((f32[4,11,2,32,256]{4,3,2,1,0:T(8,128)}), f32[4,11,2,32,256]{4,3,2,1,0:T(8,128)S(1)}, u32[]{:S(2)}, u32[]{:S(2)}) %all-to-all-start.1) | async-done | bytes 2883616 | tf_op jit(solution)/shard_map/cond/branch_1_fun/all_to_all | solution.py:77
  132.3 15.7 %all-gather.1 = f32[1,8,2,32,256]{4,3,2,0,1:T(8,128)S(1)} all-gather(f32[1,2,2,32,256]{4,3,2,0,1:T(8,128)S(1)} %dynamic-slice_bitcast_fusion.1), channel_id=3, replica_groups={{0,8,16,24},{1,9,17,25},{2,10,18,26},{3,11,19,27},{4,12,20,28},{5,13,21..., dimensions={1}, use_global_device_ids=true | all-gather | bytes 655360 | tf_op jit(solution)/shard_map/cond/branch_1_fun/all_gather | solution.py:79
  147.9 5.3 %pad_maximum_fusion.1 = f32[116,2,32,256]{3,2,1,0:T(8,128)} fusion(f32[8,2,32,256]{3,2,1,0:T(8,128)S(1)} %bitcast.196, f32[44,2,32,256]{3,2,1,0:T(8,128)S(1)} %bitcast.177, f32[64,2,32,256]{3,2,1,0:T(8,128)} %get-tuple-element.275), kind=kLoop, calls=%fused_computation.50 | loop fusion | flops 3801088 | bytes 15204352 | tf_op jit(solution)/shard_map/cond/branch_1_fun/concatenate | solution.py:80
  153.2 3.8 %gather_fusion.3 = f32[32,2,32,256]{3,2,1,0:T(8,128)S(1)} fusion(f32[116,2,32,256]{3,2,1,0:T(8,128)} %pad_maximum_fusion.1, s32[1024]{0:T(1024)S(1)} %pad_clamp_fusion.2), kind=kCustom, calls=%fused_computation.3 | custom fusion | bytes 4194432 | tf_op jit(solution)/shard_map/cond/branch_1_fun/jit(_take)/gather | solution.py:83
  157.1 1.5 broadcast_select_fusion.3
  158.6 3.2 copy.219
  161.8 5.3 %all-to-all-start.11 = ((f32[8,4,2,32,256]{4,3,1,2,0:T(8,128)}), f32[8,4,2,32,256]{4,3,1,2,0:T(8,128)S(1)}, u32[]{:S(2)}, u32[]{:S(2)}) async-start(f32[8,4,2,32,256]{4,3,1,2,0:T(8,128)} %copy.219), calls=%async_computation.11 | async-start | bytes 4194304 | tf_op jit(solution)/shard_map/all_to_all | solution.py:91
  167.8 4.2 %gather_fusion.21 = f32[4,2,256,256]{3,2,1,0:T(8,128)} fusion(f32[8,2,256,256]{3,2,1,0:T(8,128)} %param.18, s32[1024]{0:T(1024)S(1)} %pad_clamp_fusion.22), kind=kCustom, calls=%fused_computation.21 | custom fusion | bytes 4194320 | tf_op jit(solution)/shard_map/jit(_take)/gather | solution.py:104
  172.1 1.8 copy_select_fusion.1
  173.9 1.1 slice_bitcast_fusion.9
  175.0 18.7 %all-to-all-done.11 = f32[8,4,2,32,256]{4,3,1,2,0:T(8,128)S(1)} async-done(((f32[8,4,2,32,256]{4,3,1,2,0:T(8,128)}), f32[8,4,2,32,256]{4,3,1,2,0:T(8,128)S(1)}, u32[]{:S(2)}, u32[]{:S(2)}) %all-to-all-start.11) | async-done | bytes 2097184 | tf_op jit(solution)/shard_map/all_to_all | solution.py:91
  194.1 1.0 copy-done.2
  195.1 2.5 fusion.48
  197.6 1.3 slice_bitcast_fusion.12
  198.9 1.5 copy_bitcast_fusion.1
  200.4 4.3 %all-to-all-start.12 = ((f32[8,4,2,32,256]{4,3,1,2,0:T(8,128)}), f32[8,4,2,32,256]{4,3,1,2,0:T(8,128)}, u32[]{:S(2)}, u32[]{:S(2)}) async-start(f32[8,4,2,32,256]{4,3,1,2,0:T(8,128)} %copy_bitcast_fusion.1), calls=%async_computation.12 | async-start | bytes 4194304 | tf_op jit(solution)/shard_map/all_to_all | solution.py:58
  209.7 21.8 %all-to-all-done.12 = f32[8,4,2,32,256]{4,3,1,2,0:T(8,128)} async-done(((f32[8,4,2,32,256]{4,3,1,2,0:T(8,128)}), f32[8,4,2,32,256]{4,3,1,2,0:T(8,128)}, u32[]{:S(2)}, u32[]{:S(2)}) %all-to-all-start.12) | async-done | bytes 2097184 | tf_op jit(solution)/shard_map/all_to_all | solution.py:58
  231.4 1.7 copy.226
  233.2 91.8 %conditional.3 = (f32[32,2,32,256]{3,2,1,0:T(8,128)}) conditional(s32[]{:T(128)} %clamp.7, (s32[8,4]{1,0:T(8,128)S(1)}, s32[]{:T(128)}, s32[8,4]{1,0:T(8,128)S(1)}, s32[8,4]{1,0:T(8,128)S(1)}, s32[8,4]{1,0:T(8,128)S(1)}, /*index=5*/pred[8,4]{1,0:T(8,128)(4,1)S(1)}, s32[32,4]{0,1:T(4,128)S(1)}, s32[32,4]{0,1:T(4,128)S(1)}, ...), branch_computations={%region_24.26_spmd, %region_26.28_spmd, %region_28.30_spmd, %regio... | conditional | flops 8212497 | bytes 91439000 | solution.py:89
  233.8 2.2 gather_fusion.12
  236.1 3.5 broadcast_select_fusion.12
  239.5 4.6 %all-to-all-start.6 = ((f32[4,10,2,32,256]{4,3,2,1,0:T(8,128)}), f32[4,10,2,32,256]{4,3,2,1,0:T(8,128)}, u32[]{:S(2)}, u32[]{:S(2)}) async-start(f32[4,10,2,32,256]{4,3,2,1,0:T(8,128)} %broadcast_select_fusion.12), calls=%async_computation.6 | async-start | bytes 5242880 | tf_op jit(solution)/shard_map/cond/branch_1_fun/all_to_all | solution.py:77
  244.3 56.6 %all-to-all-done.6 = f32[4,10,2,32,256]{4,3,2,1,0:T(8,128)} async-done(((f32[4,10,2,32,256]{4,3,2,1,0:T(8,128)}), f32[4,10,2,32,256]{4,3,2,1,0:T(8,128)}, u32[]{:S(2)}, u32[]{:S(2)}) %all-to-all-start.6) | async-done | bytes 2621472 | tf_op jit(solution)/shard_map/cond/branch_1_fun/all_to_all | solution.py:77
  301.7 13.8 %all-gather.6 = f32[4,1,2,32,256]{4,3,2,1,0:T(8,128)S(1)} all-gather(f32[1,1,2,32,256]{4,3,2,1,0:T(8,128)S(1)} %constant_dynamic-slice_fusion.1), channel_id=8, replica_groups={{0,8,16,24},{1,9,17,25},{2,10,18,26},{3,11,19,27},{4,12,20,28},{5,13,21..., dimensions={0}, use_global_device_ids=true | all-gather | bytes 327680 | tf_op jit(solution)/shard_map/cond/branch_1_fun/all_gather | solution.py:79
  315.5 4.8 %pad_maximum_fusion.6 = f32[76,2,32,256]{3,2,1,0:T(8,128)} fusion(f32[4,2,32,256]{3,2,1,0:T(8,128)S(1)} %bitcast.200, f32[40,2,32,256]{3,2,1,0:T(8,128)} %bitcast.37, f32[32,2,32,256]{3,2,1,0:T(8,128)S(1)} %get-tuple-element.335), kind=kLoop, calls=%fused_computation.169 | loop fusion | flops 2490368 | bytes 9961472 | tf_op jit(solution)/shard_map/cond/branch_1_fun/concatenate | solution.py:80
  320.3 3.1 gather_fusion.13
  323.4 1.5 broadcast_select_fusion.13
  324.9 3.2 copy.232
  328.1 5.8 %all-to-all-start.13 = ((f32[8,4,2,32,256]{4,3,1,2,0:T(8,128)}), f32[8,4,2,32,256]{4,3,1,2,0:T(8,128)S(1)}, u32[]{:S(2)}, u32[]{:S(2)}) async-start(f32[8,4,2,32,256]{4,3,1,2,0:T(8,128)} %copy.232), calls=%async_computation.13 | async-start | bytes 4194304 | tf_op jit(solution)/shard_map/all_to_all | solution.py:91
  334.1 1.5 pad_maximum_fusion.10
  335.6 1.4 copy.221
  337.0 3.6 gather_fusion.24
  340.6 1.8 copy_select_fusion
  342.4 1.1 slice_bitcast_fusion.5
  343.6 17.0 %all-to-all-done.13 = f32[8,4,2,32,256]{4,3,1,2,0:T(8,128)S(1)} async-done(((f32[8,4,2,32,256]{4,3,1,2,0:T(8,128)}), f32[8,4,2,32,256]{4,3,1,2,0:T(8,128)S(1)}, u32[]{:S(2)}, u32[]{:S(2)}) %all-to-all-start.13) | async-done | bytes 2097184 | tf_op jit(solution)/shard_map/all_to_all | solution.py:91
  360.9 1.0 copy-done.3
  361.9 2.5 fusion.56
  365.0 1.0 pad_maximum_fusion.12
  (113 shorter events, 12.8 us)
Async XLA Ops:
  0.0 10.1 %copy-start = (s32[256]{0:T(256)S(1)}, s32[256]{0:T(256)}, u32[]{:S(2)}) copy-start(s32[256]{0:T(256)} %param.19) | copy-start | bytes 3076
  4.7 5.3 %copy-start.6 = (s32[128,2]{0,1:T(2,128)S(1)}, s32[128,2]{0,1:T(2,128)}, u32[]{:S(2)}) copy-start(s32[128,2]{0,1:T(2,128)} %param.20) | copy-start | bytes 3076
  4.7 10.1 %copy-start.4 = (s32[128,2]{0,1:T(2,128)S(1)}, s32[128,2]{0,1:T(2,128)}, u32[]{:S(2)}) copy-start(s32[128,2]{0,1:T(2,128)} %param.21) | copy-start | bytes 3076
  4.7 54.5 %all-to-all-start.10 = ((f32[8,8,2,32,256]{4,3,2,1,0:T(8,128)}), f32[8,8,2,32,256]{4,3,2,1,0:T(8,128)}, u32[]{:S(2)}, u32[]{:S(2)}) async-start(f32[8,8,2,32,256]{4,3,2,1,0:T(8,128)} %bitcast.168), calls=%async_computation.10 | async-start | bytes 8388608 | tf_op jit(solution)/shard_map/all_to_all | solution.py:58
  10.0 11.0 %copy-start.7 = (s32[4]{0:T(128)S(1)}, s32[4]{0:T(128)}, u32[]{:S(2)}) copy-start(s32[4]{0:T(128)} %constant.727.clone) | copy-start | bytes 52
  64.5 67.7 %all-to-all-start.1 = ((f32[4,11,2,32,256]{4,3,2,1,0:T(8,128)}), f32[4,11,2,32,256]{4,3,2,1,0:T(8,128)S(1)}, u32[]{:S(2)}, u32[]{:S(2)}) async-start(f32[4,11,2,32,256]{4,3,2,1,0:T(8,128)} %broadcast_select_fusion.2), calls=%async_computation.1 | async-start | bytes 5767168 | tf_op jit(solution)/shard_map/cond/branch_1_fun/all_to_all | solution.py:77
  161.8 31.9 %all-to-all-start.11 = ((f32[8,4,2,32,256]{4,3,1,2,0:T(8,128)}), f32[8,4,2,32,256]{4,3,1,2,0:T(8,128)S(1)}, u32[]{:S(2)}, u32[]{:S(2)}) async-start(f32[8,4,2,32,256]{4,3,1,2,0:T(8,128)} %copy.219), calls=%async_computation.11 | async-start | bytes 4194304 | tf_op jit(solution)/shard_map/all_to_all | solution.py:91
  167.1 4.9 %copy-start.8 = (s32[128]{0:T(128)S(1)}, s32[128]{0:T(128)}, u32[]{:S(2)}) copy-start(s32[128]{0:T(128)} %param.22) | copy-start | bytes 1540
  193.9 1.2 copy-start.2
  200.4 31.0 %all-to-all-start.12 = ((f32[8,4,2,32,256]{4,3,1,2,0:T(8,128)}), f32[8,4,2,32,256]{4,3,1,2,0:T(8,128)}, u32[]{:S(2)}, u32[]{:S(2)}) async-start(f32[8,4,2,32,256]{4,3,1,2,0:T(8,128)} %copy_bitcast_fusion.1), calls=%async_computation.12 | async-start | bytes 4194304 | tf_op jit(solution)/shard_map/all_to_all | solution.py:58
  239.5 61.4 %all-to-all-start.6 = ((f32[4,10,2,32,256]{4,3,2,1,0:T(8,128)}), f32[4,10,2,32,256]{4,3,2,1,0:T(8,128)}, u32[]{:S(2)}, u32[]{:S(2)}) async-start(f32[4,10,2,32,256]{4,3,2,1,0:T(8,128)} %broadcast_select_fusion.12), calls=%async_computation.6 | async-start | bytes 5242880 | tf_op jit(solution)/shard_map/cond/branch_1_fun/all_to_all | solution.py:77
  328.1 5.8 %copy-start.9 = (s32[128]{0:T(128)S(1)}, s32[128]{0:T(128)}, u32[]{:S(2)}) copy-start(s32[128]{0:T(128)} %param.23) | copy-start | bytes 1540
  328.1 5.8 %copy-start.5 = (s32[128,2]{0,1:T(2,128)S(1)}, s32[128,2]{0,1:T(2,128)}, u32[]{:S(2)}) copy-start(s32[128,2]{0,1:T(2,128)} %param.21) | copy-start | bytes 3076
  328.1 32.4 %all-to-all-start.13 = ((f32[8,4,2,32,256]{4,3,1,2,0:T(8,128)}), f32[8,4,2,32,256]{4,3,1,2,0:T(8,128)S(1)}, u32[]{:S(2)}, u32[]{:S(2)}) async-start(f32[8,4,2,32,256]{4,3,1,2,0:T(8,128)} %copy.232), calls=%async_computation.13 | async-start | bytes 4194304 | tf_op jit(solution)/shard_map/all_to_all | solution.py:91
  360.7 1.2 copy-start.3
  364.6 1.5 copy-start.1
